TPU v7x, 128 devices: a whole 4x4x4 slice. The times are simulated.
128 devices in a mesh: pair: 2 (over z_hi), dp: 64 (over x, y, z_lo, core).
Axes of the slice: x: 4, y: 4, z: 4 (z_hi: 2, z_lo: 2; z = z_hi * 2 + z_lo), core: 2. Of those that a mesh axis runs over, the one named last changes fastest.
Arguments:
- tokens: bfloat16 [2, 512, 128, 768], P('pair', 'dp'), may hold values from -6 to 6
- cotangent: bfloat16 [2, 512, 128, 768], P('pair', 'dp'), may hold values from -6 to 6
- span_counts: int32 [2, 64], P('pair', 'dp'), may hold values from 1 to 8, as said below
- single_flags: int32 [2, 512], P('pair', 'dp'), may hold values from 0 to 1, as said below
- partner_slots: int32 [2, 512], P('pair', 'dp'), may hold values from 0 to 7, as said below
- w_qkv: bfloat16 [768, 2304], P(('pair', 'dp')), may hold values from -0.3125 to 0.3125
- b_query: bfloat16 [768], P(('pair', 'dp')), may hold values from -3 to 3
- b_value: bfloat16 [768], P(('pair', 'dp')), may hold values from -3 to 3
- w_out: bfloat16 [768, 768], P(('pair', 'dp')), may hold values from -0.4375 to 0.4375
- b_out: bfloat16 [768], P(('pair', 'dp')), may hold values from -3 to 3
- gain_attn: bfloat16 [768], P(('pair', 'dp')), may hold values from 0.5 to 1.5
- shift_attn: bfloat16 [768], P(('pair', 'dp')), may hold values from -3 to 3
- w_in: bfloat16 [768, 3072], P(('pair', 'dp')), may hold values from -0.21875 to 0.21875
- b_in: bfloat16 [3072], P(('pair', 'dp')), may hold values from -3 to 3
- w_down: bfloat16 [3072, 768], P(('pair', 'dp')), may hold values from -0.109375 to 0.109375
- b_down: bfloat16 [768], P(('pair', 'dp')), may hold values from -3 to 3
- gain_ffn: bfloat16 [768], P(('pair', 'dp')), may hold values from 0.5 to 1.5
- shift_ffn: bfloat16 [768], P(('pair', 'dp')), may hold values from -3 to 3
Outputs:
- mixed: bfloat16 [2, 512, 128, 768], P('pair', 'dp')
- grad_tokens: bfloat16 [2, 512, 128, 768], P('pair', 'dp')
- grad_w_qkv: float32 [768, 2304], P(('pair', 'dp'))
- grad_b_query: float32 [768], P(('pair', 'dp'))
- grad_b_value: float32 [768], P(('pair', 'dp'))
- grad_w_out: float32 [768, 768], P(('pair', 'dp'))
- grad_b_out: float32 [768], P(('pair', 'dp'))
- grad_gain_attn: float32 [768], P(('pair', 'dp'))
- grad_shift_attn: float32 [768], P(('pair', 'dp'))
- grad_w_in: float32 [768, 3072], P(('pair', 'dp'))
- grad_b_in: float32 [3072], P(('pair', 'dp'))
- grad_w_down: float32 [3072, 768], P(('pair', 'dp'))
- grad_b_down: float32 [768], P(('pair', 'dp'))
- grad_gain_ffn: float32 [768], P(('pair', 'dp'))
- grad_shift_ffn: float32 [768], P(('pair', 'dp'))
Inputs may be any that keep to these rules, and one draw needn't show every extreme that they name: `span_counts`: live slots of a device are slots 0 to count - 1; in every draw some device holds 8 live spans. `single_flags`: 1 only for a live span whose document has a single span; 0 for paired spans and empty slots; both sides of a dp index hold equally many paired spans. `partner_slots`: for a paired span, the slot of its partner on the other side at the same dp index, whose partner is it again; for any other slot, the slot itself.
All inputs are finite; a program needn't handle non-finite values.
Results may differ from a plain program's by a relative error of at most 0.015.
The roundings to bfloat16 on the way count: a program that leaves them out, or rounds other values in their place, can miss the bound.
Values may be sent and summed in bfloat16 or wider, within the bound.
No kernel may reach another device: no remote copies, remote signals or barrier semaphores. Data moves between devices by JAX's collectives and lax.ppermute only.
A program may use at most 192 MiB of HBM per device.

v0:
```python
import jax
import jax.numpy as jnp
from jax import lax
from jax.sharding import PartitionSpec as P

HEADS = 12
HEAD_DIM = 64


epsilon = 1e-12
contrast_weight = 8.0
logit_scale = 0.0625


def from_partner(value, axis, bit):
    mask = 2**bit
    pairs = [(source, source ^ mask) for source in range(lax.axis_size(axis))]
    return lax.ppermute(value, axis, pairs)


def layer_norm(resid, gain, shift):
    centered = resid - jnp.mean(resid, axis=-1, keepdims=True)
    variance = jnp.mean(centered * centered, axis=-1, keepdims=True)
    return centered * lax.rsqrt(variance + epsilon) * gain + shift


def gelu_exact(upper):
    return 0.5 * upper * (1.0 + jax.scipy.special.erf(upper * 0.7071067811865476))


def contrast(first, received, keep, partner):
    logits = jnp.dot(first, received.T, precision=lax.Precision.HIGHEST) * logit_scale
    totals = jax.nn.logsumexp(logits, axis=-1)
    picked = jnp.take_along_axis(logits, partner[:, None], axis=-1)[:, 0]
    return contrast_weight * jnp.sum(keep * (totals - picked))


def outer_sum(left, right):
    return jnp.einsum("ti,to->io", left, right, preferred_element_type=jnp.float32)


def per_device(
    tokens,
    cotangent,
    span_counts,
    single_flags,
    partner_slots,
    w_qkv,
    b_query,
    b_value,
    w_out,
    b_out,
    gain_attn,
    shift_attn,
    w_in,
    b_in,
    w_down,
    b_down,
    gain_ffn,
    shift_ffn,
):
    spans = tokens.shape[1]
    span_len = tokens.shape[2]
    width = tokens.shape[3]
    f32 = jnp.float32
    bf16 = jnp.bfloat16
    scale = HEAD_DIM ** (-0.5)
    full = (
        lax.all_gather(w_qkv, ("pair", "dp"), axis=0, tiled=True),
        lax.all_gather(b_query, ("pair", "dp"), axis=0, tiled=True),
        lax.all_gather(b_value, ("pair", "dp"), axis=0, tiled=True),
        lax.all_gather(w_out, ("pair", "dp"), axis=0, tiled=True),
        lax.all_gather(b_out, ("pair", "dp"), axis=0, tiled=True),
        lax.all_gather(gain_attn, ("pair", "dp"), axis=0, tiled=True),
        lax.all_gather(shift_attn, ("pair", "dp"), axis=0, tiled=True),
        lax.all_gather(w_in, ("pair", "dp"), axis=0, tiled=True),
        lax.all_gather(b_in, ("pair", "dp"), axis=0, tiled=True),
        lax.all_gather(w_down, ("pair", "dp"), axis=0, tiled=True),
        lax.all_gather(b_down, ("pair", "dp"), axis=0, tiled=True),
        lax.all_gather(gain_ffn, ("pair", "dp"), axis=0, tiled=True),
        lax.all_gather(shift_ffn, ("pair", "dp"), axis=0, tiled=True),
    )
    (
        fw_qkv,
        fb_query,
        fb_value,
        fw_out,
        fb_out,
        fgain_attn,
        fshift_attn,
        fw_in,
        fb_in,
        fw_down,
        fb_down,
        fgain_ffn,
        fshift_ffn,
    ) = full
    slot = jnp.arange(spans, dtype=jnp.int32)
    live = (slot < span_counts[0, 0]).astype(f32)
    keep = live * (1.0 - single_flags[0].astype(f32))
    partner = partner_slots[0]
    rows = tokens.reshape(-1, width)
    bias = jnp.concatenate([fb_query.astype(f32), jnp.zeros((width,), f32), fb_value.astype(f32)])
    qkv = (jnp.dot(rows, fw_qkv, preferred_element_type=f32) + bias).astype(bf16)
    qkv_heads = qkv.reshape(spans, span_len, 3, HEADS, HEAD_DIM)
    query, keyed, valued = (qkv_heads[:, :, 0], qkv_heads[:, :, 1], qkv_heads[:, :, 2])
    scores = jnp.einsum("sqhd,skhd->shqk", query, keyed, preferred_element_type=f32) * scale
    totals = jax.nn.logsumexp(scores, axis=-1)
    probs_low = jnp.exp(scores - totals[..., None]).astype(bf16)
    heads_out = jnp.einsum("shqk,skhd->sqhd", probs_low, valued, preferred_element_type=f32)
    heads_out = heads_out.reshape(-1, width).astype(bf16)
    attn = jnp.dot(heads_out, fw_out, preferred_element_type=f32) + fb_out.astype(f32)
    hidden_one, norm_one_pull = jax.vjp(
        layer_norm, rows.astype(f32) + attn, fgain_attn.astype(f32), fshift_attn.astype(f32)
    )
    hidden_low = hidden_one.astype(bf16)
    upper = jnp.dot(hidden_low, fw_in, preferred_element_type=f32) + fb_in.astype(f32)
    active_f, gelu_pull = jax.vjp(gelu_exact, upper)
    active = active_f.astype(bf16)
    down = jnp.dot(active, fw_down, preferred_element_type=f32) + fb_down.astype(f32)
    final, norm_two_pull = jax.vjp(
        layer_norm, hidden_one + down, fgain_ffn.astype(f32), fshift_ffn.astype(f32)
    )
    final_grid = final.reshape(spans, span_len, width)
    mixed = (final_grid * live[:, None, None]).astype(bf16)
    first = final_grid[:, 0, :]
    sent = (first.astype(bf16).astype(f32) * keep[:, None]).astype(bf16)
    received = from_partner(sent, "pair", 0)
    loss_value, loss_pull = jax.vjp(
        lambda mine, theirs: contrast(mine, theirs, keep, partner), first, received.astype(f32)
    )
    dfirst, dreceived = loss_pull(jnp.ones((), f32))
    returned = from_partner(dreceived.astype(bf16), "pair", 0)
    dsent = returned.astype(f32) * keep[:, None]
    back = (
        lax.all_gather(w_qkv, ("pair", "dp"), axis=0, tiled=True),
        lax.all_gather(b_query, ("pair", "dp"), axis=0, tiled=True),
        lax.all_gather(b_value, ("pair", "dp"), axis=0, tiled=True),
        lax.all_gather(w_out, ("pair", "dp"), axis=0, tiled=True),
        lax.all_gather(b_out, ("pair", "dp"), axis=0, tiled=True),
        lax.all_gather(gain_attn, ("pair", "dp"), axis=0, tiled=True),
        lax.all_gather(shift_attn, ("pair", "dp"), axis=0, tiled=True),
        lax.all_gather(w_in, ("pair", "dp"), axis=0, tiled=True),
        lax.all_gather(b_in, ("pair", "dp"), axis=0, tiled=True),
        lax.all_gather(w_down, ("pair", "dp"), axis=0, tiled=True),
        lax.all_gather(b_down, ("pair", "dp"), axis=0, tiled=True),
        lax.all_gather(gain_ffn, ("pair", "dp"), axis=0, tiled=True),
        lax.all_gather(shift_ffn, ("pair", "dp"), axis=0, tiled=True),
    )
    bw_qkv, bw_out, bw_in, bw_down = (back[0], back[3], back[7], back[9])
    dfinal = cotangent.reshape(spans, span_len, width).astype(f32) * live[:, None, None]
    dfinal = dfinal.at[:, 0, :].add(dfirst + dsent)
    dres2, dgain_ffn, dshift_ffn = norm_two_pull(dfinal.reshape(-1, width))
    ddown = dres2.astype(bf16)
    db_down = jnp.sum(ddown.astype(f32), axis=0)
    dw_down = outer_sum(active, ddown)
    dactive = jnp.dot(ddown, bw_down.T, preferred_element_type=f32)
    (dupper_f,) = gelu_pull(dactive)
    dupper = dupper_f.astype(bf16)
    db_in = jnp.sum(dupper.astype(f32), axis=0)
    dw_in = outer_sum(hidden_low, dupper)
    dhidden = dres2 + jnp.dot(dupper, bw_in.T, preferred_element_type=f32)
    dres1, dgain_attn, dshift_attn = norm_one_pull(dhidden)
    dattn = dres1.astype(bf16)
    db_out = jnp.sum(dattn.astype(f32), axis=0)
    dw_out = outer_sum(heads_out, dattn)
    dheads = jnp.dot(dattn, bw_out.T, preferred_element_type=f32).astype(bf16)
    dheads = dheads.reshape(spans, span_len, HEADS, HEAD_DIM)
    again_scores = jnp.einsum("sqhd,skhd->shqk", query, keyed, preferred_element_type=f32) * scale
    probs = jnp.exp(again_scores - totals[..., None])
    dprobs = jnp.einsum("sqhd,skhd->shqk", dheads, valued, preferred_element_type=f32)
    dvalue = jnp.einsum("shqk,sqhd->skhd", probs.astype(bf16), dheads, preferred_element_type=f32)
    inner = jnp.sum(probs * dprobs, axis=-1, keepdims=True)
    dscores = (probs * (dprobs - inner)).astype(bf16)
    dquery = jnp.einsum("shqk,skhd->sqhd", dscores, keyed, preferred_element_type=f32) * scale
    dkey = jnp.einsum("shqk,sqhd->skhd", dscores, query, preferred_element_type=f32) * scale
    dqkv = jnp.stack([dquery, dkey, dvalue], axis=2).reshape(-1, 3 * width).astype(bf16)
    dqkv_f = dqkv.astype(f32)
    db_query = jnp.sum(dqkv_f[:, :width], axis=0)
    db_value = jnp.sum(dqkv_f[:, 2 * width :], axis=0)
    dw_qkv = outer_sum(rows, dqkv)
    grad_rows = dres1 + jnp.dot(dqkv, bw_qkv.T, preferred_element_type=f32)
    grad_tokens = grad_rows.reshape(tokens.shape).astype(bf16)
    parts = (
        lax.psum_scatter(dw_qkv, ("pair", "dp"), scatter_dimension=0, tiled=True),
        lax.psum_scatter(db_query, ("pair", "dp"), scatter_dimension=0, tiled=True),
        lax.psum_scatter(db_value, ("pair", "dp"), scatter_dimension=0, tiled=True),
        lax.psum_scatter(dw_out, ("pair", "dp"), scatter_dimension=0, tiled=True),
        lax.psum_scatter(db_out, ("pair", "dp"), scatter_dimension=0, tiled=True),
        lax.psum_scatter(dgain_attn, ("pair", "dp"), scatter_dimension=0, tiled=True),
        lax.psum_scatter(dshift_attn, ("pair", "dp"), scatter_dimension=0, tiled=True),
        lax.psum_scatter(dw_in, ("pair", "dp"), scatter_dimension=0, tiled=True),
        lax.psum_scatter(db_in, ("pair", "dp"), scatter_dimension=0, tiled=True),
        lax.psum_scatter(dw_down, ("pair", "dp"), scatter_dimension=0, tiled=True),
        lax.psum_scatter(db_down, ("pair", "dp"), scatter_dimension=0, tiled=True),
        lax.psum_scatter(dgain_ffn, ("pair", "dp"), scatter_dimension=0, tiled=True),
        lax.psum_scatter(dshift_ffn, ("pair", "dp"), scatter_dimension=0, tiled=True),
    )
    return (
        mixed.reshape(tokens.shape),
        grad_tokens,
        parts[0],
        parts[1],
        parts[2],
        parts[3],
        parts[4],
        parts[5],
        parts[6],
        parts[7],
        parts[8],
        parts[9],
        parts[10],
        parts[11],
        parts[12],
    )


def solution(mesh):
    return jax.shard_map(
        per_device,
        mesh=mesh,
        in_specs=(
            P("pair", "dp", None, None),
            P("pair", "dp", None, None),
            P("pair", "dp"),
            P("pair", "dp"),
            P("pair", "dp"),
            P(("pair", "dp"), None),
            P(("pair", "dp")),
            P(("pair", "dp")),
            P(("pair", "dp"), None),
            P(("pair", "dp")),
            P(("pair", "dp")),
            P(("pair", "dp")),
            P(("pair", "dp"), None),
            P(("pair", "dp")),
            P(("pair", "dp"), None),
            P(("pair", "dp")),
            P(("pair", "dp")),
            P(("pair", "dp")),
        ),
        out_specs=(
            P("pair", "dp", None, None),
            P("pair", "dp", None, None),
            P(("pair", "dp"), None),
            P(("pair", "dp")),
            P(("pair", "dp")),
            P(("pair", "dp"), None),
            P(("pair", "dp")),
            P(("pair", "dp")),
            P(("pair", "dp")),
            P(("pair", "dp"), None),
            P(("pair", "dp")),
            P(("pair", "dp"), None),
            P(("pair", "dp")),
            P(("pair", "dp")),
            P(("pair", "dp")),
        ),
        check_vma=False,
    )
```

profile of v0, /device:TPU:0, one launch (start us, length us, event | category | flops | bytes accessed | tf_op | source)
XLA Modules:
  0.0 1736.2 jit_solution(14165166394822758666)
XLA Ops:
  18.2 68.8 %all-reduce.24 = (bf16[768]{0:T(1024)(128)(2,1)S(1)}, bf16[768]{0:T(1024)(128)(2,1)S(1)}, bf16[768]{0:T(1024)(128)(2,1)S(1)}, bf16[768]{0:T(1024)(128)(2,1)S(1)}...) all-reduce(bf16[768]{0:T(1024)(128)(2,1)S(1)} %dynamic-update-slice, ...), channel_id=1, replica_groups=mesh['pair'=2,'dp'=64] {'pair','dp'}, use_global_device_ids=true, to_apply=%add.2 | all-reduce | flops 9216 | bytes 36864
  91.8 114.1 %all-gather.12.cloned.1.call-done = bf16[128,6,768]{2,1,0:T(8,128)(2,1)} async-done(((bf16[1,6,768]{2,1,0:T(8,128)(2,1)}), bf16[128,6,768]{2,1,0:T(8,128)(2,1)}) %all-gather.12.cloned.1.call-update) | async-done | bytes 1179664 | tf_op jit(solution)/shard_map/all_gather | solution.py:72
  209.1 196.6 %all-gather.10.cloned.1.call-done = bf16[128,6,2304]{2,1,0:T(8,128)(2,1)} async-done(((bf16[1,6,2304]{2,1,0:T(8,128)(2,1)}), bf16[128,6,2304]{2,1,0:T(8,128)(2,1)}) %all-gather.10.cloned.1.call-update) | async-done | bytes 3538960 | tf_op jit(solution)/shard_map/all_gather | solution.py:69
  410.8 8.6 add_convert_fusion.1
  419.4 6.8 copy.63
  439.7 167.5 %all-gather.14.cloned.1.call-done = bf16[128,6,3072]{2,1,0:T(8,128)(2,1)} async-done(((bf16[1,6,3072]{2,1,0:T(8,128)(2,1)}), bf16[128,6,3072]{2,1,0:T(8,128)(2,1)}) %all-gather.14.cloned.1.call-update) | async-done | bytes 4718608 | tf_op jit(solution)/shard_map/all_gather | solution.py:76
  607.2 7.8 reshape.274
  615.0 12.1 multiply_convert_fusion
  627.2 179.9 %all-gather.8.cloned.1.call-done = bf16[3072,768]{1,0:T(8,128)(2,1)} async-done(((bf16[24,768]{1,0:T(8,128)(2,1)}), bf16[3072,768]{1,0:T(8,128)(2,1)}) %all-gather.8.cloned.1.call-update) | async-done | bytes 4718608 | tf_op jit(solution)/shard_map/all_gather | solution.py:78
  807.1 9.0 fusion.60
  835.3 15.2 convert_reduce_fusion
  850.4 6.4 multiply_reduce_fusion.2
  887.2 9.3 copy.78
  898.6 5.8 convolution_bitcast_fusion
  904.4 10.4 fusion.62
  919.6 10.8 fusion.51
  930.4 365.8 %fusion.55 = (f32[8,768]{1,0:T(8,128)S(1)}, f32[8,3072]{1,0:T(8,128)S(1)}) fusion(f32[768,768]{1,0:T(8,128)} %fusion.12, f32[768,3072]{1,0:T(8,128)} %fusion.51), kind=kCustom, calls=%all-reduce-scatter.2 | all-reduce-scatter fusion | flops 3932161 | bytes 11919360
  1308.2 18.3 %collective-permute-start.24 = (f32[8,768]{1,0:T(8,128)S(1)}, f32[8,768]{1,0:T(8,128)S(1)}, u32[]{:S(2)}, u32[]{:S(2)}) collective-permute-start(f32[8,768]{1,0:T(8,128)S(1)} %get-tuple-element.99), channel_id=1, source_target_pairs={{0,23},{1,24},{2,25},{3,26},{4,27},{5,28},{6,29},{7,30},{8,31},{9,... | collective-permute-start | bytes 73736
  1341.8 6.2 collective-permute-start.16
  1452.4 5.9 collective-permute-start.43
  1471.8 63.2 %all-reduce.23 = (f32[768]{0:T(1024)S(1)}, f32[768]{0:T(1024)S(1)}, f32[768]{0:T(1024)S(1)}, f32[768]{0:T(1024)S(1)}, f32[768]{0:T(1024)S(1)}, /*index=5*/f32[30...) all-reduce(f32[768]{0:T(1024)S(1)} %get-tuple-element.73, ...), channel_id=3, replica_groups=mesh['pair'=2,'dp'=64] {'pair','dp'}, use_global_device_ids=true, to_apply=%region_15.16.clone | all-reduce | flops 9216 | bytes 73728
  1540.2 24.9 %concatenate.6 = f32[262,768]{1,0:T(8,128)S(1)} concatenate(f32[6,768]{1,0:T(8,128)} %copy-done.44, f32[8,768]{1,0:T(8,128)S(1)} %collective-permute-done.32, f32[8,768]{1,0:T(8,128)S(1)} %collective-permute-done.31, f32[8,768]{1,0:T(8,128)S(1)} %copy-done.43, f32[8,768]{1,0:T(8,128)} %copy-done.45, f32[8,768]{1,0:T(8,128)} %copy-done.46, f32[8,768]{1,0:T(8,128)} %copy-done.47, ...), dimensions={0} | concatenate | bytes 1609728
  1585.5 31.5 %concatenate.7 = f32[262,3072]{1,0:T(8,128)S(1)} concatenate(f32[6,3072]{1,0:T(8,128)S(1)} %collective-permute-done.65, f32[8,3072]{1,0:T(8,128)S(1)} %collective-permute-done.64, f32[8,3072]{1,0:T(8,128)} %collective-permute-done.63, f32[8,3072]{1,0:T(8,128)} %collective-permute-done.62, f32[8,3072]{1,0:T(8,128)} %collective-permute-done.61, f32[8,3072]{1,0:T(8,128)} %collective-permute-done.60, ...), dimensions={0} | concatenate | bytes 6438912
  1620.7 108.5 %reduce-scatter.7.cloned.1.call-done = f32[24,768]{1,0:T(8,128)} async-done(((f32[3072,768]{1,0:T(8,128)}), f32[24,768]{1,0:T(8,128)}) %reduce-scatter.7.cloned.1.call-update) | async-done | bytes 73744 | tf_op jit(solution)/shard_map/reduce_scatter | solution.py:194
  (429 shorter events, 265.8 us)
Async XLA Ops:
  7.2 198.7 %all-gather.12.cloned.1.call-start = ((), (), s32[]{:S(2)}) async-start(), calls=%async_computation.4 | async-start | bytes 1585152 | tf_op jit(solution)/shard_map/all_gather | solution.py:72
  7.9 397.8 %all-gather.10.cloned.1.call-start = ((), (), s32[]{:S(2)}) async-start(), calls=%async_computation.3 | async-start | bytes 4755456 | tf_op jit(solution)/shard_map/all_gather | solution.py:69
  8.7 598.6 %all-gather.14.cloned.1.call-start = ((), (), s32[]{:S(2)}) async-start(), calls=%async_computation.5 | async-start | bytes 6340608 | tf_op jit(solution)/shard_map/all_gather | solution.py:76
  9.4 797.7 %all-gather.8.cloned.1.call-start = ((), (), s32[]{:S(2)}) async-start(), calls=%async_computation.1 | async-start | bytes 4755456 | tf_op jit(solution)/shard_map/all_gather | solution.py:78
  10.0 1607.7 %all-reduce.28.cloned.1.call-start = ((), (), s32[]{:S(2)}) async-start(), calls=%async_computation.6 | async-start | bytes 14155776
  904.4 824.8 %reduce-scatter.7.cloned.1.call-start = ((), (), s32[]{:S(2)}) async-start(), calls=%async_computation.2 | async-start | bytes 9510912 | tf_op jit(solution)/shard_map/reduce_scatter | solution.py:194
  1303.0 23.5 %collective-permute-start.28 = (f32[8,768]{1,0:T(8,128)S(1)}, f32[8,768]{1,0:T(8,128)S(1)}, u32[]{:S(2)}, u32[]{:S(2)}) collective-permute-start(f32[8,768]{1,0:T(8,128)S(1)} %get-tuple-element.99), channel_id=1, source_target_pairs={{0,27},{1,28},{2,29},{3,30},{4,31},{5,32},{6,33},{7,34},{8,35},{9,... | collective-permute-start | bytes 73736
  1304.3 26.9 %collective-permute-start.27 = (f32[8,768]{1,0:T(8,128)S(1)}, f32[8,768]{1,0:T(8,128)S(1)}, u32[]{:S(2)}, u32[]{:S(2)}) collective-permute-start(f32[8,768]{1,0:T(8,128)S(1)} %get-tuple-element.99), channel_id=1, source_target_pairs={{0,26},{1,27},{2,28},{3,29},{4,30},{5,31},{6,32},{7,33},{8,34},{9,... | collective-permute-start | bytes 73736
  1305.6 26.9 %collective-permute-start.26 = (f32[8,768]{1,0:T(8,128)S(1)}, f32[8,768]{1,0:T(8,128)S(1)}, u32[]{:S(2)}, u32[]{:S(2)}) collective-permute-start(f32[8,768]{1,0:T(8,128)S(1)} %get-tuple-element.99), channel_id=1, source_target_pairs={{0,25},{1,26},{2,27},{3,28},{4,29},{5,30},{6,31},{7,32},{8,33},{9,... | collective-permute-start | bytes 73736
  1306.9 27.0 %collective-permute-start.25 = (f32[8,768]{1,0:T(8,128)S(1)}, f32[8,768]{1,0:T(8,128)S(1)}, u32[]{:S(2)}, u32[]{:S(2)}) collective-permute-start(f32[8,768]{1,0:T(8,128)S(1)} %get-tuple-element.99), channel_id=1, source_target_pairs={{0,24},{1,25},{2,26},{3,27},{4,28},{5,29},{6,30},{7,31},{8,32},{9,... | collective-permute-start | bytes 73736
  1308.2 28.5 %collective-permute-start.24 = (f32[8,768]{1,0:T(8,128)S(1)}, f32[8,768]{1,0:T(8,128)S(1)}, u32[]{:S(2)}, u32[]{:S(2)}) collective-permute-start(f32[8,768]{1,0:T(8,128)S(1)} %get-tuple-element.99), channel_id=1, source_target_pairs={{0,23},{1,24},{2,25},{3,26},{4,27},{5,28},{6,29},{7,30},{8,31},{9,... | collective-permute-start | bytes 73736
  1360.1 40.4 %collective-permute-start.64 = (f32[8,3072]{1,0:T(8,128)S(1)}, f32[8,3072]{1,0:T(8,128)S(1)}, u32[]{:S(2)}, u32[]{:S(2)}) collective-permute-start(f32[8,3072]{1,0:T(8,128)S(1)} %get-tuple-element.100), channel_id=1, source_target_pairs={{0,31},{1,32},{2,33},{3,34},{4,35},{5,36},{6,37},{7,38},{8,39},{9,... | collective-permute-start | bytes 294920
  1370.5 27.2 %collective-permute-start.65 = (f32[6,3072]{1,0:T(8,128)S(1)}, f32[6,3072]{1,0:T(8,128)S(1)}, u32[]{:S(2)}, u32[]{:S(2)}) collective-permute-start(f32[6,3072]{1,0:T(8,128)S(1)} %slice.55), channel_id=1, source_target_pairs={{0,32},{1,33},{2,34},{3,35},{4,36},{5,37},{6,38},{7,39},{8,40},{9,... | collective-permute-start | bytes 221192
  1422.7 17.8 %collective-permute-start.51 = (f32[8,3072]{1,0:T(8,128)S(1)}, f32[8,3072]{1,0:T(8,128)S(1)}, u32[]{:S(2)}, u32[]{:S(2)}) collective-permute-start(f32[8,3072]{1,0:T(8,128)S(1)} %get-tuple-element.100), channel_id=1, source_target_pairs={{0,18},{1,19},{2,20},{3,21},{4,22},{5,23},{6,24},{7,25},{8,26},{9,... | collective-permute-start | bytes 294920
  1432.6 19.8 %collective-permute-start.48 = (f32[8,3072]{1,0:T(8,128)S(1)}, f32[8,3072]{1,0:T(8,128)S(1)}, u32[]{:S(2)}, u32[]{:S(2)}) collective-permute-start(f32[8,3072]{1,0:T(8,128)S(1)} %get-tuple-element.100), channel_id=1, source_target_pairs={{0,15},{1,16},{2,17},{3,18},{4,19},{5,20},{6,21},{7,22},{8,23},{9,... | collective-permute-start | bytes 294920
  1437.5 20.8 %collective-permute-start.47 = (f32[8,3072]{1,0:T(8,128)S(1)}, f32[8,3072]{1,0:T(8,128)S(1)}, u32[]{:S(2)}, u32[]{:S(2)}) collective-permute-start(f32[8,3072]{1,0:T(8,128)S(1)} %get-tuple-element.100), channel_id=1, source_target_pairs={{0,14},{1,15},{2,16},{3,17},{4,18},{5,19},{6,20},{7,21},{8,22},{9,... | collective-permute-start | bytes 294920
  1440.5 20.4 %collective-permute-start.46 = (f32[8,3072]{1,0:T(8,128)S(1)}, f32[8,3072]{1,0:T(8,128)S(1)}, u32[]{:S(2)}, u32[]{:S(2)}) collective-permute-start(f32[8,3072]{1,0:T(8,128)S(1)} %get-tuple-element.100), channel_id=1, source_target_pairs={{0,13},{1,14},{2,15},{3,16},{4,17},{5,18},{6,19},{7,20},{8,21},{9,... | collective-permute-start | bytes 294920
  1442.7 21.3 %collective-permute-start.45 = (f32[8,3072]{1,0:T(8,128)S(1)}, f32[8,3072]{1,0:T(8,128)S(1)}, u32[]{:S(2)}, u32[]{:S(2)}) collective-permute-start(f32[8,3072]{1,0:T(8,128)S(1)} %get-tuple-element.100), channel_id=1, source_target_pairs={{0,12},{1,13},{2,14},{3,15},{4,16},{5,17},{6,18},{7,19},{8,20},{9,... | collective-permute-start | bytes 294920
  1444.6 21.7 %collective-permute-start.44 = (f32[8,3072]{1,0:T(8,128)S(1)}, f32[8,3072]{1,0:T(8,128)S(1)}, u32[]{:S(2)}, u32[]{:S(2)}) collective-permute-start(f32[8,3072]{1,0:T(8,128)S(1)} %get-tuple-element.100), channel_id=1, source_target_pairs={{0,11},{1,12},{2,13},{3,14},{4,15},{5,16},{6,17},{7,18},{8,19},{9,... | collective-permute-start | bytes 294920
  1452.4 112.7 %collective-permute-start.43 = (f32[8,3072]{1,0:T(8,128)S(1)}, f32[8,3072]{1,0:T(8,128)}, u32[]{:S(2)}, u32[]{:S(2)}) collective-permute-start(f32[8,3072]{1,0:T(8,128)S(1)} %get-tuple-element.100), channel_id=1, source_target_pairs={{0,10},{1,11},{2,12},{3,13},{4,14},{5,15},{6,16},{7,17},{8,18},{9,... | collective-permute-start | bytes 294920
  1458.3 109.0 %collective-permute-start.42 = (f32[8,3072]{1,0:T(8,128)S(1)}, f32[8,3072]{1,0:T(8,128)}, u32[]{:S(2)}, u32[]{:S(2)}) collective-permute-start(f32[8,3072]{1,0:T(8,128)S(1)} %get-tuple-element.100), channel_id=1, source_target_pairs={{0,9},{1,10},{2,11},{3,12},{4,13},{5,14},{6,15},{7,16},{8,17},{9,1... | collective-permute-start | bytes 294920
  1460.9 109.3 %collective-permute-start.41 = (f32[8,3072]{1,0:T(8,128)S(1)}, f32[8,3072]{1,0:T(8,128)}, u32[]{:S(2)}, u32[]{:S(2)}) collective-permute-start(f32[8,3072]{1,0:T(8,128)S(1)} %get-tuple-element.100), channel_id=1, source_target_pairs={{0,8},{1,9},{2,10},{3,11},{4,12},{5,13},{6,14},{7,15},{8,16},{9,17... | collective-permute-start | bytes 294920
  1464.0 111.4 %collective-permute-start.40 = (f32[8,3072]{1,0:T(8,128)S(1)}, f32[8,3072]{1,0:T(8,128)}, u32[]{:S(2)}, u32[]{:S(2)}) collective-permute-start(f32[8,3072]{1,0:T(8,128)S(1)} %get-tuple-element.100), channel_id=1, source_target_pairs={{0,7},{1,8},{2,9},{3,10},{4,11},{5,12},{6,13},{7,14},{8,15},{9,16}... | collective-permute-start | bytes 294920
  1466.3 110.5 %collective-permute-start.39 = (f32[8,3072]{1,0:T(8,128)S(1)}, f32[8,3072]{1,0:T(8,128)}, u32[]{:S(2)}, u32[]{:S(2)}) collective-permute-start(f32[8,3072]{1,0:T(8,128)S(1)} %get-tuple-element.100), channel_id=1, source_target_pairs={{0,6},{1,7},{2,8},{3,9},{4,10},{5,11},{6,12},{7,13},{8,14},{9,15},... | collective-permute-start | bytes 294920
  (140 other events, 3247.6 us)
Sparse Core Ops, SparseCore 0:
  9.7 196.0 all-gather.11
  207.6 198.0 all-gather.9
  407.4 199.7 all-gather.13
  608.8 198.2 all-gather.7
  904.5 164.7 all-reduce.27
  1072.2 656.9 reduce-scatter.6
where the time goes:
time: 1750 us; the launch traced here: 1740 us
  waiting for transfers between devices  779 us (45%)
  blocking collectives  498 us (28%)
  starting transfers between devices  180 us (10%)
  local copies, waits for them, and re-layouts  126 us (7%)
  matrix products  108 us (6%)
  other arithmetic  27.7 us (2%)
    unnamed x3, blocking collectives  498 us
    all_gather x1, waiting for transfers between devices, per_device(): lax.all_gather(w_qkv, ('pair', 'dp'), axis=0, tiled=True)  197 us
    all_gather x1, waiting for transfers between devices, per_device(): lax.all_gather(w_down, ('pair', 'dp'), axis=0, tiled=True)  180 us
    unnamed x65, starting transfers between devices  176 us
    all_gather x1, waiting for transfers between devices, per_device(): lax.all_gather(w_in, ('pair', 'dp'), axis=0, tiled=True)  168 us
    all_gather x1, waiting for transfers between devices, per_device(): lax.all_gather(w_out, ('pair', 'dp'), axis=0, tiled=True)  114 us
    reduce_scatter x1, waiting for transfers between devices, per_device(): lax.psum_scatter(dw_down, ('pair', 'dp'), scatter_dimension=0, tiled=True)  108 us
    unnamed x224, local copies, waits for them, and re-layouts  105 us
  transfers between devices with their start and end apart: 72, of which 10 were waited for; matrix products, arithmetic and copies ran while one was open for 31% of the time, Pallas kernels for 0%

commit v1 on v0

--- a/solution.py
+++ b/solution.py
@@ -1,6 +1,10 @@
+import functools
+
 import jax
 import jax.numpy as jnp
 from jax import lax
+from jax.experimental import pallas as pl
+from jax.experimental.pallas import tpu as pltpu
 from jax.sharding import PartitionSpec as P
 
 HEADS = 12
@@ -10,7 +14,6 @@
 epsilon = 1e-12
 contrast_weight = 8.0
 logit_scale = 0.0625
-
 
 def from_partner(value, axis, bit):
     mask = 2**bit
@@ -37,6 +40,174 @@
 
 def outer_sum(left, right):
     return jnp.einsum("ti,to->io", left, right, preferred_element_type=jnp.float32)
+
+
+AXES = ("pair", "dp")
+UNIT = 48
+
+
+def device_index(p, a, yh, yl, z, c):
+    return ((((p * 4 + a) * 2 + yh) * 2 + yl) * 2 + z) * 2 + c
+
+
+def all_places():
+    return [
+        (p, a, yh, yl, z, c)
+        for p in range(2)
+        for a in range(4)
+        for yh in range(2)
+        for yl in range(2)
+        for z in range(2)
+        for c in range(2)
+    ]
+
+
+def moved(place, stage, r):
+    p, a, yh, yl, z, c = place
+    if (stage == 0) == (c == 0):
+        return (p ^ (r & 1), a, yh ^ (r >> 1), yl, z, c)
+    return (p, (a + r) % 4, yh, yl, z, c)
+
+
+def stage_pairs(stage, r, back=False):
+    pairs = [(device_index(*moved(q, stage, r)), device_index(*q)) for q in all_places()]
+    return [(t, s) for s, t in pairs] if back else pairs
+
+
+def core_pairs():
+    return [(d, d ^ 1) for d in range(128)]
+
+
+def octets():
+    return [[8 * g + k for k in range(8)] for g in range(16)]
+
+
+def send(value, pairs):
+    return lax.ppermute(value, AXES, pairs)
+
+
+def exchange_octet(value):
+    return lax.all_to_all(value, AXES, 0, 0, axis_index_groups=octets(), tiled=True)
+
+
+def my_units():
+    me = lax.axis_index("pair") * 64 + lax.axis_index("dp")
+    c, yh, a, p = me & 1, (me >> 3) & 1, (me >> 4) & 3, me >> 6
+    i = jnp.arange(16, dtype=jnp.int32)
+    late, early = i >> 2, i & 3
+    zero = (p ^ (early & 1)) * 8 + ((a + late) & 3) * 2 + (yh ^ (early >> 1))
+    one = (p ^ (late & 1)) * 8 + ((a + early) & 3) * 2 + (yh ^ (late >> 1))
+    return c, jnp.stack([zero, one]).astype(jnp.int32)
+
+
+WIDE = (1152, 128, 384)
+FIRST = sum(WIDE)
+SECOND = 3072
+
+
+def gather_stage(block, stage):
+    return jnp.stack([block] + [send(block, stage_pairs(stage, r)) for r in (1, 2, 3)])
+
+
+def gather_pieces(block):
+    early = gather_stage(block, 0)
+    mine = [early] + [send(early, stage_pairs(1, r)) for r in (1, 2, 3)]
+    theirs = [send(piece, core_pairs()) for piece in mine]
+    return mine, theirs
+
+
+def place_kernel(layout, n_out, place, *refs):
+    pieces, outs, sems = refs[:8], refs[8 : 8 + n_out], refs[8 + n_out]
+    core = place[0]
+    for side in range(2):
+        half = core if side == 0 else 1 - core
+        for k in range(16):
+            unit = place[1 + half * 16 + k]
+            block = pieces[4 * side + k // 4].at[k % 4]
+            for n, (first, width, times) in enumerate(layout):
+                to = pl.ds(pl.multiple_of(half * width, 128), width)
+                for j in range(times):
+                    pltpu.make_async_copy(
+                        block.at[:, pl.ds(first + j * width, width)],
+                        outs[n].at[pl.ds(pl.multiple_of((unit * times + j) * UNIT, 16), UNIT), to],
+                        sems.at[side, n],
+                    ).start()
+    for side in range(2):
+        half = core if side == 0 else 1 - core
+        for n, (first, width, times) in enumerate(layout):
+            whole = outs[n].at[:, pl.ds(pl.multiple_of(half * width, 128), width)]
+            pltpu.make_async_copy(whole, whole, sems.at[side, n]).wait()
+
+
+def place_weights(place, mine, theirs, layout):
+    shapes = [jax.ShapeDtypeStruct((768 * t, 2 * w), jnp.bfloat16) for _, w, t in layout]
+    return pl.pallas_call(
+        functools.partial(place_kernel, layout, len(layout)),
+        out_shape=shapes,
+        in_specs=[pl.BlockSpec(memory_space=pltpu.SMEM)] + [pl.BlockSpec(memory_space=pl.ANY)] * 8,
+        out_specs=[pl.BlockSpec(memory_space=pltpu.VMEM)] * len(layout),
+        scratch_shapes=[pltpu.SemaphoreType.DMA((2, len(layout)))],
+        compiler_params=pltpu.CompilerParams(vmem_limit_bytes=40 * 2**20),
+    )(place, *mine, *theirs)
+
+
+def split_kernel(layout, total, place, *refs):
+    n_in = len(layout)
+    grads, outs, sems = refs[:n_in], refs[n_in : n_in + 2], refs[n_in + 2]
+    core = place[0]
+    for side in range(2):
+        half = core if side == 0 else 1 - core
+        for k in range(16):
+            unit = place[1 + half * 16 + k]
+            for n, (first, width, times) in enumerate(layout):
+                here = pl.ds(pl.multiple_of(half * width, 128), width)
+                for j in range(times):
+                    pltpu.make_async_copy(
+                        grads[n].at[pl.ds(pl.multiple_of((unit * times + j) * UNIT, 16), UNIT), here],
+                        outs[side].at[k, :, pl.ds(first + j * width, width)],
+                        sems.at[side],
+                    ).start()
+    for side in range(2):
+        pltpu.make_async_copy(outs[side], outs[side], sems.at[side]).wait()
+
+
+def split_grads(place, grads, layout):
+    total = sum(w * t for _, w, t in layout)
+    shape = jax.ShapeDtypeStruct((16, UNIT, total), jnp.bfloat16)
+    return pl.pallas_call(
+        functools.partial(split_kernel, layout, total),
+        out_shape=[shape, shape],
+        in_specs=[pl.BlockSpec(memory_space=pltpu.SMEM)] + [pl.BlockSpec(memory_space=pltpu.VMEM)] * len(grads),
+        out_specs=[pl.BlockSpec(memory_space=pl.ANY)] * 2,
+        scratch_shapes=[pltpu.SemaphoreType.DMA((2,))],
+        compiler_params=pltpu.CompilerParams(vmem_limit_bytes=40 * 2**20),
+    )(place, *grads)
+
+
+def add_low(parts):
+    total = parts[0].astype(jnp.float32)
+    for part in parts[1:]:
+        total = total + part.astype(jnp.float32)
+    return total.astype(jnp.bfloat16)
+
+
+def scatter_stage(blocks, stage):
+    return add_low([blocks[0]] + [send(blocks[r], stage_pairs(stage, r, True)) for r in (1, 2, 3)])
+
+
+def scatter_pieces(mine, theirs):
+    total = add_low([mine, send(theirs, core_pairs())])
+    total = total.reshape(4, 4, UNIT, -1)
+    return scatter_stage(scatter_stage(total, 1), 0)
+
+
+LAYOUT_ONE = ((0, 1152, 1), (1152, 128, 1), (1280, 384, 1))
+LAYOUT_TWO = ((0, 1536, 1), (1536, 384, 4))
+
+
+def halves(value):
+    width = value.shape[1] // 2
+    return value[:, :width], value[:, width:]
 
 
 def per_device(
@@ -65,36 +236,42 @@
     f32 = jnp.float32
     bf16 = jnp.bfloat16
     scale = HEAD_DIM ** (-0.5)
-    full = (
-        lax.all_gather(w_qkv, ("pair", "dp"), axis=0, tiled=True),
-        lax.all_gather(b_query, ("pair", "dp"), axis=0, tiled=True),
-        lax.all_gather(b_value, ("pair", "dp"), axis=0, tiled=True),
-        lax.all_gather(w_out, ("pair", "dp"), axis=0, tiled=True),
-        lax.all_gather(b_out, ("pair", "dp"), axis=0, tiled=True),
-        lax.all_gather(gain_attn, ("pair", "dp"), axis=0, tiled=True),
-        lax.all_gather(shift_attn, ("pair", "dp"), axis=0, tiled=True),
-        lax.all_gather(w_in, ("pair", "dp"), axis=0, tiled=True),
-        lax.all_gather(b_in, ("pair", "dp"), axis=0, tiled=True),
-        lax.all_gather(w_down, ("pair", "dp"), axis=0, tiled=True),
-        lax.all_gather(b_down, ("pair", "dp"), axis=0, tiled=True),
-        lax.all_gather(gain_ffn, ("pair", "dp"), axis=0, tiled=True),
-        lax.all_gather(shift_ffn, ("pair", "dp"), axis=0, tiled=True),
-    )
-    (
-        fw_qkv,
-        fb_query,
-        fb_value,
-        fw_out,
-        fb_out,
-        fgain_attn,
-        fshift_attn,
-        fw_in,
-        fb_in,
-        fw_down,
-        fb_down,
-        fgain_ffn,
-        fshift_ffn,
-    ) = full
+    core, units = my_units()
+    place = jnp.concatenate([core[None], units.reshape(-1)]).astype(jnp.int32)
+    vectors = jnp.concatenate(
+        [
+            jnp.stack([b_query, b_value, b_out, gain_attn, shift_attn, b_down, gain_ffn, shift_ffn], axis=1),
+            b_in.reshape(6, 4),
+            jnp.zeros((6, 116), bf16),
+        ],
+        axis=1,
+    )
+    packed = []
+    for h in range(2):
+        packed.append(
+            jnp.concatenate(
+                [
+                    halves(w_qkv)[h],
+                    vectors,
+                    halves(w_out)[h],
+                    halves(w_in)[h],
+                    halves(w_down)[h].reshape(6, 1536),
+                ],
+                axis=1,
+            )
+        )
+    rows48 = exchange_octet(jnp.stack(packed * 4))
+    one = rows48[:, :, :FIRST].reshape(UNIT, FIRST)
+    two_in = rows48[:, :, FIRST : FIRST + 1536].reshape(UNIT, 1536)
+    two_down = rows48[:, :, FIRST + 1536 :].reshape(4, UNIT, 384).transpose(1, 0, 2).reshape(UNIT, 1536)
+    two = jnp.concatenate([two_in, two_down], axis=1)
+    fw_qkv, fvectors, fw_out = place_weights(place, *gather_pieces(one), LAYOUT_ONE)
+    fw_in, fw_down = place_weights(place, *gather_pieces(two), LAYOUT_TWO)
+    fvectors = fvectors[:, :12]
+    fb_query, fb_value, fb_out, fgain_attn, fshift_attn, fb_down, fgain_ffn, fshift_ffn = [
+        fvectors[:, i] for i in range(8)
+    ]
+    fb_in = fvectors[:, 8:12].reshape(-1)
     slot = jnp.arange(spans, dtype=jnp.int32)
     live = (slot < span_counts[0, 0]).astype(f32)
     keep = live * (1.0 - single_flags[0].astype(f32))
@@ -132,22 +309,7 @@
     dfirst, dreceived = loss_pull(jnp.ones((), f32))
     returned = from_partner(dreceived.astype(bf16), "pair", 0)
     dsent = returned.astype(f32) * keep[:, None]
-    back = (
-        lax.all_gather(w_qkv, ("pair", "dp"), axis=0, tiled=True),
-        lax.all_gather(b_query, ("pair", "dp"), axis=0, tiled=True),
-        lax.all_gather(b_value, ("pair", "dp"), axis=0, tiled=True),
-        lax.all_gather(w_out, ("pair", "dp"), axis=0, tiled=True),
-        lax.all_gather(b_out, ("pair", "dp"), axis=0, tiled=True),
-        lax.all_gather(gain_attn, ("pair", "dp"), axis=0, tiled=True),
-        lax.all_gather(shift_attn, ("pair", "dp"), axis=0, tiled=True),
-        lax.all_gather(w_in, ("pair", "dp"), axis=0, tiled=True),
-        lax.all_gather(b_in, ("pair", "dp"), axis=0, tiled=True),
-        lax.all_gather(w_down, ("pair", "dp"), axis=0, tiled=True),
-        lax.all_gather(b_down, ("pair", "dp"), axis=0, tiled=True),
-        lax.all_gather(gain_ffn, ("pair", "dp"), axis=0, tiled=True),
-        lax.all_gather(shift_ffn, ("pair", "dp"), axis=0, tiled=True),
-    )
-    bw_qkv, bw_out, bw_in, bw_down = (back[0], back[3], back[7], back[9])
+    bw_qkv, bw_out, bw_in, bw_down = fw_qkv, fw_out, fw_in, fw_down
     dfinal = cotangent.reshape(spans, span_len, width).astype(f32) * live[:, None, None]
     dfinal = dfinal.at[:, 0, :].add(dfirst + dsent)
     dres2, dgain_ffn, dshift_ffn = norm_two_pull(dfinal.reshape(-1, width))
@@ -181,37 +343,42 @@
     dw_qkv = outer_sum(rows, dqkv)
     grad_rows = dres1 + jnp.dot(dqkv, bw_qkv.T, preferred_element_type=f32)
     grad_tokens = grad_rows.reshape(tokens.shape).astype(bf16)
-    parts = (
-        lax.psum_scatter(dw_qkv, ("pair", "dp"), scatter_dimension=0, tiled=True),
-        lax.psum_scatter(db_query, ("pair", "dp"), scatter_dimension=0, tiled=True),
-        lax.psum_scatter(db_value, ("pair", "dp"), scatter_dimension=0, tiled=True),
-        lax.psum_scatter(dw_out, ("pair", "dp"), scatter_dimension=0, tiled=True),
-        lax.psum_scatter(db_out, ("pair", "dp"), scatter_dimension=0, tiled=True),
-        lax.psum_scatter(dgain_attn, ("pair", "dp"), scatter_dimension=0, tiled=True),
-        lax.psum_scatter(dshift_attn, ("pair", "dp"), scatter_dimension=0, tiled=True),
-        lax.psum_scatter(dw_in, ("pair", "dp"), scatter_dimension=0, tiled=True),
-        lax.psum_scatter(db_in, ("pair", "dp"), scatter_dimension=0, tiled=True),
-        lax.psum_scatter(dw_down, ("pair", "dp"), scatter_dimension=0, tiled=True),
-        lax.psum_scatter(db_down, ("pair", "dp"), scatter_dimension=0, tiled=True),
-        lax.psum_scatter(dgain_ffn, ("pair", "dp"), scatter_dimension=0, tiled=True),
-        lax.psum_scatter(dshift_ffn, ("pair", "dp"), scatter_dimension=0, tiled=True),
-    )
+    dvectors = jnp.stack(
+        [db_query, db_value, db_out, dgain_attn, dshift_attn, db_down, dgain_ffn, dshift_ffn], axis=1
+    )
+    dvectors = jnp.concatenate(
+        [dvectors, db_in.reshape(768, 4), jnp.zeros((768, 244), f32)], axis=1
+    ).astype(bf16)
+    two = scatter_pieces(*split_grads(place, [dw_in.astype(bf16), dw_down.astype(bf16)], LAYOUT_TWO))
+    one = scatter_pieces(
+        *split_grads(place, [dw_qkv.astype(bf16), dvectors, dw_out.astype(bf16)], LAYOUT_ONE)
+    )
+    two_down = two[:, 1536:].reshape(UNIT, 4, 384).transpose(1, 0, 2).reshape(8, 6, 1536)
+    back = jnp.concatenate([one.reshape(8, 6, FIRST), two[:, :1536].reshape(8, 6, 1536), two_down], axis=2)
+    back = exchange_octet(back).reshape(4, 2, 6, -1)
+    sums = jnp.sum(back.astype(f32), axis=0)
+
+    def joined(first, width):
+        return jnp.concatenate([sums[0, :, first : first + width], sums[1, :, first : first + width]], axis=1)
+
+    own = sums[0, :, 1152:1164]
+    own_down = jnp.concatenate([sums[h, :, FIRST + 1536 :].reshape(24, 384) for h in range(2)], axis=1)
     return (
         mixed.reshape(tokens.shape),
         grad_tokens,
-        parts[0],
-        parts[1],
-        parts[2],
-        parts[3],
-        parts[4],
-        parts[5],
-        parts[6],
-        parts[7],
-        parts[8],
-        parts[9],
-        parts[10],
-        parts[11],
-        parts[12],
+        joined(0, 1152),
+        own[:, 0],
+        own[:, 1],
+        joined(1280, 384),
+        own[:, 2],
+        own[:, 3],
+        own[:, 4],
+        joined(FIRST, 1536),
+        own[:, 8:12].reshape(24),
+        own_down,
+        own[:, 5],
+        own[:, 6],
+        own[:, 7],
     )
 
 

time: 1750 us -> 360 us (0.21)
  waiting for transfers between devices: 779 us -> 69.8 us
  blocking collectives: 498 us -> 0 us
  starting transfers between devices: 180 us -> 68.1 us
  local copies, waits for them, and re-layouts: 126 us -> 52.3 us
    all_gather x4 -> x0, waiting for transfers between devices: 658 us -> none  [the longest x1 197 us: per_device(): lax.all_gather(w_qkv, ('pair', 'dp'), axis=0, tiled=True)]
    unnamed x3 -> x0, blocking collectives: 498 us -> none
    unnamed x65 -> x0, starting transfers between devices: 176 us -> none
    reduce_scatter x1 -> x0, waiting for transfers between devices: 108 us -> none  [per_device(): lax.psum_scatter(dw_down, ('pair', 'dp'), scatter_dimension=0, tiled=True)]
    unnamed x224 -> x68, local copies, waits for them, and re-layouts: 105 us -> 12.3 us
    ppermute x0 -> x34, starting transfers between devices: none -> 54.4 us  [send(): return lax.ppermute(value, AXES, pairs)]
    ppermute x0 -> x34, waiting for transfers between devices: none -> 53.7 us  [send(): return lax.ppermute(value, AXES, pairs)]
  transfers between devices with their start and end apart: 72 -> 38, of which waited for: 10 -> 21; matrix products, arithmetic and copies ran while one was open for 31% -> 17% of each run, Pallas kernels for 0% -> 1%
where the time goes in v1:
time: 360 us; the launch traced here: 353 us
  matrix products  99.8 us (28%)
  waiting for transfers between devices  69.8 us (19%)
  starting transfers between devices  68.1 us (19%)
  local copies, waits for them, and re-layouts  52.3 us (15%)
  other arithmetic  45 us (12%)
  Pallas kernels  15.5 us (4%)
    ppermute x34, starting transfers between devices, send(): return lax.ppermute(value, AXES, pairs)  54.4 us
    ppermute x34, waiting for transfers between devices, send(): return lax.ppermute(value, AXES, pairs)  53.7 us
    dot_general x4, matrix products, outer_sum(): jnp.einsum('ti,to->io', left, right, preferred_element_type=jnp.float32)  24.9 us
    dot_general x1, matrix products, per_device(): dactive = jnp.dot(ddown, bw_down.T, preferred_element_type=f32)  14 us
    unnamed x68, local copies, waits for them, and re-layouts  12.3 us
    all_to_all x2, waiting for transfers between devices, exchange_octet(): lax.all_to_all(value, AXES, 0, 0, axis_index_groups=octets(), tiled=True)  11.4 us
    convert_element_type x1, local copies, waits for them, and re-layouts, per_device(): jnp.stack([dquery, dkey, dvalue], axis=2).reshape(-1, 3 * width)  9.3 us
    dot_general x1, matrix products, per_device(): jnp.dot(hidden_low, fw_in, preferred_element_type=f32) + fb_in.astype(f32)  8.97 us
  transfers between devices with their start and end apart: 38, of which 21 were waited for; matrix products, arithmetic and copies ran while one was open for 17% of the time, Pallas kernels for 1%

profile of v1, /device:TPU:0, one launch (start us, length us, event | category | flops | bytes accessed | tf_op | source)
XLA Modules:
  0.0 352.9 jit_solution(10926643801855876557)
XLA Ops:
  20.1 9.7 %all-to-all-done = bf16[8,6,4736]{2,1,0:T(8,128)(2,1)S(1)} async-done(((bf16[8,6,4736]{2,1,0:T(8,128)(2,1)}), bf16[8,6,4736]{2,1,0:T(8,128)(2,1)S(1)}, u32[]{:S(2)}, u32[]{:S(2)}) %all-to-all-start) | async-done | bytes 454688 | tf_op jit(solution)/shard_map/all_to_all | solution.py:90
  29.9 6.0 %collective-permute-start.2 = (bf16[48,1664]{1,0:T(8,128)(2,1)S(1)}, bf16[48,1664]{1,0:T(8,128)(2,1)S(1)}, u32[]{:S(2)}, u32[]{:S(2)}) collective-permute-start(bf16[48,1664]{1,0:T(8,128)(2,1)S(1)} %reshape.441), channel_id=1, source_target_pairs={{72,0},{49,1},{74,2},{51,3},{76,4},{53,5},{78,6},{55,7},{64,8},{57... | collective-permute-start | bytes 479240 | tf_op jit(solution)/shard_map/ppermute | solution.py:86
  53.5 8.2 %collective-permute-done.12 = bf16[48,3072]{1,0:T(8,128)(2,1)S(1)} collective-permute-done((bf16[48,3072]{1,0:T(8,128)(2,1)S(1)}, bf16[48,3072]{1,0:T(8,128)(2,1)S(1)}, u32[]{:S(2)}, u32[]{:S(2)}) %collective-permute-start.12) | collective-permute-done | bytes 294944 | tf_op jit(solution)/shard_map/ppermute | solution.py:86
  79.4 5.1 %fusion.11 = bf16[288,8,8,128]{3,1,2,0:T(8,128)(2,1)S(1)} fusion(f32[2304]{0:T(1024)S(1)} %pad_maximum_fusion.7, bf16[768,2304]{1,0:T(8,128)(2,1)S(1)} %get-tuple-element.36, bf16[1024,768]{1,0:T(8,128)(2,1)S(1)} %bitcast.247), kind=kOutput, calls=%fused_computation.49 | convolution fusion | flops 3628597248 | bytes 9839616 | tf_op jit(solution)/shard_map/dot_general | solution.py:281
  91.5 4.7 %exponential_reduce_fusion = f32[8,12,128]{2,1,0:T(8,128)S(1)} fusion(f32[8,12,128,128]{2,3,1,0:T(8,128)} %get-tuple-element.114, f32[8,12,128]{2,1,0:T(8,128)S(1)} %is-finite_select_fusion), kind=kLoop, calls=%fused_computation.9 | loop fusion | flops 4706304 | bytes 6389760 | tf_op jit(solution)/shard_map/reduce_sum | solution.py:285
  107.3 5.2 %shard_map.290 = (bf16[768,3072]{1,0:T(8,128)(2,1)S(1)}, bf16[3072,768]{1,0:T(8,128)(2,1)}) custom-call(s32[33]{0:T(128)S(1)} %pad_add_fusion.1.place, bf16[4,48,3072]{2,1,0:T(8,128)(2,1)S(1)} %pad_maximum_fusion.refs_0_, bf16[4,48,3072]{2,1,0:T(8,128)(2,1)} %collective-permute-done.13.refs_1_, bf16[4,48,3072]{2,1,0:T(8,128)(2,1)} %collective-permute-done.14.refs_2_, ...), custom_call_target="tpu_custom_call" | custom-call | tf_op jit(solution)/shard_map/pallas_call | solution.py:144
  112.5 9.0 %multiply_convert_fusion = (bf16[1024,3072]{1,0:T(8,128)(2,1)S(1)}, f32[1024,3072]{1,0:T(8,128)}) fusion(f32[3072]{0:T(1024)S(1)} %reshape.462, bf16[768,3072]{1,0:T(8,128)(2,1)S(1)} %get-tuple-element.39, f32[1024,768]{1,0:T(8,128)S(1)} %get-tuple-element.116, f32[768]{0:T(1024)S(1)} %get-tuple-element.55, f32[768]{0:T(1024)S(1)} %get-tuple-element.56, ...), kind=kOutput, calls=%fused_computation.1 | convolution fusion | flops 4854644736 | bytes 26765312 | tf_op jit(solution)/shard_map/dot_general | solution.py:294
  121.4 5.3 %fusion.80 = (f32[1024]{0:T(1024)S(1)}, f32[1024,768]{1,0:T(8,128)S(1)}) fusion(f32[768]{0:T(1024)S(1)} %get-tuple-element.54, bf16[1024,3072]{1,0:T(8,128)(2,1)S(1)} %get-tuple-element.117, bf16[3072,768]{1,0:T(8,128)(2,1)S(1)} %copy-done.19, f32[768]{0:T(1024)S(1)} %get-tuple-element.55, f32[768]{0:T(1024)S(1)} %get-tuple-element.56, ...), kind=kOutput, calls=%fused_computation.202 | convolution fusion | flops 4837342208 | bytes 17323008 | tf_op jit(solution)/shard_map/dot_general | solution.py:297
  145.0 6.9 %convolution_convert_fusion.refs_1_ = bf16[3072,768]{1,0:T(8,128)(2,1)} fusion(bf16[1024,3072]{1,0:T(8,128)(2,1)S(1)} %get-tuple-element.117, bf16[1024,768]{1,0:T(8,128)(2,1)S(1)} %get-tuple-element.69), kind=kOutput, calls=%fused_computation.12 | convolution fusion | flops 4834197504 | bytes 12582912 | tf_op jit(solution)/shard_map/ti,to->io/dot_general | solution.py:42
  151.8 14.0 %fusion.82 = (bf16[3072]{0:T(1024)(128)(2,1)S(1)}, bf16[1024,3072]{1,0:T(8,128)(2,1)}) fusion(bf16[1024,768]{1,0:T(8,128)(2,1)S(1)} %get-tuple-element.69, bf16[3072,768]{1,0:T(8,128)(2,1)S(1)} %copy-done.19, f32[1024,3072]{1,0:T(8,128)} %get-tuple-element.118, f32[3072]{0:T(1024)S(1)} %reshape.462), kind=kOutput, calls=%fused_computation.204 | convolution fusion | flops 4879021056 | bytes 25184256 | tf_op jit(solution)/shard_map/dot_general | solution.py:319
  165.8 8.1 %multiply_reduce_fusion.2 = (bf16[768]{0:T(1024)(128)(2,1)S(1)}, f32[1024]{0:T(1024)S(1)}, bf16[768]{0:T(1024)(128)(2,1)S(1)}, f32[1024,768]{1,0:T(8,128)S(1)}) fusion(f32[1024,768]{1,0:T(8,128)S(1)} %get-tuple-element.116, f32[1024]{0:T(1024)S(1)} %fusion.39, f32[1024]{0:T(1024)S(1)} %broadcast_multiply_fusion.1, f32[768]{0:T(1024)S(1)} %get-tuple-element.56, ...), kind=kOutput, calls=%fused_computation.31 | convolution fusion | flops 4839699456 | bytes 20469760 | tf_op jit(solution)/shard_map/dot_general | solution.py:324
  173.9 9.9 %convolution_convert_fusion.1.refs_0_ = bf16[768,3072]{1,0:T(8,128)(2,1)} fusion(bf16[1024,3072]{1,0:T(8,128)(2,1)} %get-tuple-element.127, f32[1024,768]{1,0:T(8,128)S(1)} %get-tuple-element.116, f32[768]{0:T(1024)S(1)} %get-tuple-element.55, f32[768]{0:T(1024)S(1)} %get-tuple-element.56, f32[1024]{0:T(1024)S(1)} %fusion.39, ...), kind=kOutput, calls=%fused_computation.13 | convolution fusion | flops 4838129664 | bytes 14170112 | tf_op jit(solution)/shard_map/ti,to->io/dot_general | solution.py:42
  191.9 5.2 %convolution_bitcast_fusion = bf16[8,128,1,12,64]{1,4,3,0,2:T(8,128)(2,1)S(1)} fusion(bf16[8,128,12,64]{1,0,3,2:T(8,128)(2,1)S(1)} %bitcast.220, f32[8,12,128,128]{2,3,1,0:T(8,128)} %get-tuple-element.114, f32[8,12,128]{2,1,0:T(8,128)S(1)} %log_add_fusion), kind=kOutput, calls=%fused_computation.50 | convolution fusion | flops 206045184 | bytes 9486336 | tf_op jit(solution)/shard_map/shqk,sqhd->skhd/dot_general | solution.py:334
  197.1 5.7 %multiply_reduce_fusion = (f32[8,12,128]{2,1,0:T(8,128)S(1)}, f32[8,12,128,128]{2,3,1,0:T(8,128)}) fusion(f32[8,12,128,128]{2,3,1,0:T(8,128)} %get-tuple-element.114, f32[8,12,128]{2,1,0:T(8,128)S(1)} %log_add_fusion, bf16[8,128,1,12,64]{1,0,4,3,2:T(8,128)(2,1)S(1)} %copy-done.12, bf16[8,128,12,64]{1,0,3,2:T(8,128)(2,1)S(1)} %bitcast.221), kind=kOutput, calls=%fused_computation.7 | convolution fusion | flops 207605760 | bytes 15826944 | tf_op jit(solution)/shard_map/sqhd,skhd->shqk/dot_general | solution.py:333
  202.8 4.7 %multiply_convert_fusion.1 = bf16[8,12,128,128]{2,3,1,0:T(8,128)(2,1)S(1)} fusion(f32[8,12,128,128]{2,3,1,0:T(8,128)} %get-tuple-element.125, f32[8,12,128,128]{2,3,1,0:T(8,128)S(1)} %bitcast.215, f32[8,12,128]{2,1,0:T(8,128)S(1)} %get-tuple-element.124, f32[8,12,128]{2,1,0:T(8,128)S(1)} %log_add_fusion), kind=kLoop, calls=%fused_computation.6 | loop fusion | flops 7864320 | bytes 15826944 | tf_op jit(solution)/shard_map/convert_element_type | solution.py:336
  211.8 9.3 %copy.94 = bf16[8,128,3,12,64]{1,0,4,3,2:T(8,128)(2,1)S(1)} copy(bf16[8,128,3,12,64]{1,4,3,0,2:T(8,128)(2,1)S(1)} %maximum_convert_fusion) | data formatting | bytes 9437184 | tf_op jit(solution)/shard_map/convert_element_type | solution.py:339
  223.3 5.3 %bitcast_convert_fusion = f32[1024,2304]{0,1:T(8,128)} fusion(bf16[288,8,8,128]{3,2,1,0:T(8,128)(2,1)S(1)} %bitcast.216), kind=kLoop, calls=%fused_computation.17 | loop fusion | flops 2359296 | bytes 14155776 | tf_op jit(solution)/shard_map/convert_element_type | solution.py:340
  228.6 6.0 %shard_map.292 = (bf16[16,48,3072]{2,1,0:T(8,128)(2,1)S(1)}, bf16[16,48,3072]{2,1,0:T(8,128)(2,1)}) custom-call(s32[33]{0:T(128)S(1)} %pad_add_fusion.1.place, bf16[768,3072]{1,0:T(8,128)(2,1)S(1)} %bitcast.213, bf16[3072,768]{1,0:T(8,128)(2,1)} %convolution_convert_fusion.refs_1_), custom_call_target="tpu_custom_call" | custom-call | tf_op jit(solution)/shard_map/pallas_call | solution.py:177
  246.9 6.7 %fusion.3.refs_0_ = bf16[768,2304]{1,0:T(8,128)(2,1)S(1)} fusion(bf16[1024,768]{1,0:T(8,128)(2,1)} %bitcast.246, bf16[288,8,8,128]{3,2,1,0:T(8,128)(2,1)} %bitcast.217), kind=kOutput, calls=%fused_computation.21 | convolution fusion | flops 3625648128 | bytes 9830400 | tf_op jit(solution)/shard_map/ti,to->io/dot_general | solution.py:42
  256.2 4.4 %collective-permute-done.22 = bf16[16,48,1664]{2,1,0:T(8,128)(2,1)S(1)} collective-permute-done((bf16[16,48,1664]{2,1,0:T(8,128)(2,1)S(1)}, bf16[16,48,1664]{2,1,0:T(8,128)(2,1)S(1)}, u32[]{:S(2)}, u32[]{:S(2)}) %collective-permute-start.22) | collective-permute-done | bytes 2555936 | tf_op jit(solution)/shard_map/ppermute | solution.py:86
  287.0 7.8 %collective-permute-done.30 = bf16[4,48,3072]{2,1,0:T(8,128)(2,1)S(1)} collective-permute-done((bf16[4,48,3072]{2,1,0:T(8,128)(2,1)S(1)}, bf16[4,48,3072]{2,1,0:T(8,128)(2,1)S(1)}, u32[]{:S(2)}, u32[]{:S(2)}) %collective-permute-start.30) | collective-permute-done | bytes 1179680 | tf_op jit(solution)/shard_map/ppermute | solution.py:86
  297.7 9.8 %collective-permute-done.31 = bf16[4,48,3072]{2,1,0:T(8,128)(2,1)S(1)} collective-permute-done((bf16[4,48,3072]{2,1,0:T(8,128)(2,1)S(1)}, bf16[4,48,3072]{2,1,0:T(8,128)(2,1)S(1)}, u32[]{:S(2)}, u32[]{:S(2)}) %collective-permute-start.31) | collective-permute-done | bytes 1179680 | tf_op jit(solution)/shard_map/ppermute | solution.py:86
  309.2 4.9 %collective-permute-start.33 = (bf16[48,3072]{1,0:T(8,128)(2,1)}, bf16[48,3072]{1,0:T(8,128)(2,1)}, u32[]{:S(2)}, u32[]{:S(2)}) collective-permute-start(bf16[48,3072]{1,0:T(8,128)(2,1)} %get-tuple-element.87), channel_id=1, source_target_pairs={{0,64},{1,17},{2,66},{3,19},{4,68},{5,21},{6,70},{7,23},{8,72},{9,... | collective-permute-start | bytes 884744 | tf_op jit(solution)/shard_map/ppermute | solution.py:86
  337.6 8.0 %add_convert_fusion.4 = bf16[1024,768]{1,0:T(8,128)(2,1)} fusion(f32[1024,768]{1,0:T(8,128)} %copy-done.15, bf16[768,2304]{1,0:T(8,128)(2,1)S(1)} %copy-done.2, bf16[288,8,8,128]{3,2,1,0:T(8,128)(2,1)} %bitcast.218, f32[1024]{0:T(1024)S(1)} %negate_multiply_fusion), kind=kOutput, calls=%fused_computation.32 | convolution fusion | flops 3626237952 | bytes 12980224 | tf_op jit(solution)/shard_map/dot_general | solution.py:344
  (266 shorter events, 180.6 us)
Async XLA Ops:
  15.8 14.0 %all-to-all-start = ((bf16[8,6,4736]{2,1,0:T(8,128)(2,1)}), bf16[8,6,4736]{2,1,0:T(8,128)(2,1)S(1)}, u32[]{:S(2)}, u32[]{:S(2)}) async-start(bf16[8,6,4736]{2,1,0:T(8,128)(2,1)} %bitcast_dynamic-update-slice_fusion.3), calls=%async_computation | async-start | bytes 1212416 | tf_op jit(solution)/shard_map/all_to_all | solution.py:90
  43.4 21.9 %collective-permute-start.5 = (bf16[4,48,1664]{2,1,0:T(8,128)(2,1)S(1)}, bf16[4,48,1664]{2,1,0:T(8,128)(2,1)}, u32[]{:S(2)}, u32[]{:S(2)}) collective-permute-start(bf16[4,48,1664]{2,1,0:T(8,128)(2,1)S(1)} %pad_maximum_fusion.1.refs_0_), channel_id=1, source_target_pairs={{48,0},{73,1},{50,2},{75,3},{52,4},{77,5},{54,6},{79,7},{56,8},{65... | collective-permute-start | bytes 1916936 | tf_op jit(solution)/shard_map/ppermute | solution.py:86
  44.9 23.9 %collective-permute-start.4 = (bf16[4,48,1664]{2,1,0:T(8,128)(2,1)S(1)}, bf16[4,48,1664]{2,1,0:T(8,128)(2,1)}, u32[]{:S(2)}, u32[]{:S(2)}) collective-permute-start(bf16[4,48,1664]{2,1,0:T(8,128)(2,1)S(1)} %pad_maximum_fusion.1.refs_0_), channel_id=1, source_target_pairs={{32,0},{9,1},{34,2},{11,3},{36,4},{13,5},{38,6},{15,7},{40,8},{1,9... | collective-permute-start | bytes 1916936 | tf_op jit(solution)/shard_map/ppermute | solution.py:86
  47.6 21.2 %collective-permute-start.3 = (bf16[4,48,1664]{2,1,0:T(8,128)(2,1)S(1)}, bf16[4,48,1664]{2,1,0:T(8,128)(2,1)}, u32[]{:S(2)}, u32[]{:S(2)}) collective-permute-start(bf16[4,48,1664]{2,1,0:T(8,128)(2,1)S(1)} %pad_maximum_fusion.1.refs_0_), channel_id=1, source_target_pairs={{16,0},{65,1},{18,2},{67,3},{20,4},{69,5},{22,6},{71,7},{24,8},{73... | collective-permute-start | bytes 1916936 | tf_op jit(solution)/shard_map/ppermute | solution.py:86
  49.2 12.5 %collective-permute-start.12 = (bf16[48,3072]{1,0:T(8,128)(2,1)S(1)}, bf16[48,3072]{1,0:T(8,128)(2,1)S(1)}, u32[]{:S(2)}, u32[]{:S(2)}) collective-permute-start(bf16[48,3072]{1,0:T(8,128)(2,1)S(1)} %constant_dynamic-update-slice_fusion), channel_id=1, source_target_pairs={{72,0},{49,1},{74,2},{51,3},{76,4},{53,5},{78,6},{55,7},{64,8},{57... | collective-permute-start | bytes 884744 | tf_op jit(solution)/shard_map/ppermute | solution.py:86
  52.8 12.4 %collective-permute-start.11 = (bf16[48,3072]{1,0:T(8,128)(2,1)S(1)}, bf16[48,3072]{1,0:T(8,128)(2,1)S(1)}, u32[]{:S(2)}, u32[]{:S(2)}) collective-permute-start(bf16[48,3072]{1,0:T(8,128)(2,1)S(1)} %constant_dynamic-update-slice_fusion), channel_id=1, source_target_pairs={{8,0},{33,1},{10,2},{35,3},{12,4},{37,5},{14,6},{39,7},{0,8},{41,9... | collective-permute-start | bytes 884744 | tf_op jit(solution)/shard_map/ppermute | solution.py:86
  70.3 34.4 %collective-permute-start.16 = (bf16[4,48,3072]{2,1,0:T(8,128)(2,1)S(1)}, bf16[4,48,3072]{2,1,0:T(8,128)(2,1)S(1)}, u32[]{:S(2)}, u32[]{:S(2)}) collective-permute-start(bf16[4,48,3072]{2,1,0:T(8,128)(2,1)S(1)} %pad_maximum_fusion.refs_0_), channel_id=1, source_target_pairs={{0,1},{1,0},{2,3},{3,2},{4,5},{5,4},{6,7},{7,6},{8,9},{9,8},{10,11... | collective-permute-start | bytes 3538952 | tf_op jit(solution)/shard_map/ppermute | solution.py:86
  70.4 29.8 %collective-permute-start.15 = (bf16[4,48,3072]{2,1,0:T(8,128)(2,1)S(1)}, bf16[4,48,3072]{2,1,0:T(8,128)(2,1)}, u32[]{:S(2)}, u32[]{:S(2)}) collective-permute-start(bf16[4,48,3072]{2,1,0:T(8,128)(2,1)S(1)} %pad_maximum_fusion.refs_0_), channel_id=1, source_target_pairs={{48,0},{73,1},{50,2},{75,3},{52,4},{77,5},{54,6},{79,7},{56,8},{65... | collective-permute-start | bytes 3538952 | tf_op jit(solution)/shard_map/ppermute | solution.py:86
  72.4 29.0 %collective-permute-start.14 = (bf16[4,48,3072]{2,1,0:T(8,128)(2,1)S(1)}, bf16[4,48,3072]{2,1,0:T(8,128)(2,1)}, u32[]{:S(2)}, u32[]{:S(2)}) collective-permute-start(bf16[4,48,3072]{2,1,0:T(8,128)(2,1)S(1)} %pad_maximum_fusion.refs_0_), channel_id=1, source_target_pairs={{32,0},{9,1},{34,2},{11,3},{36,4},{13,5},{38,6},{15,7},{40,8},{1,9... | collective-permute-start | bytes 3538952 | tf_op jit(solution)/shard_map/ppermute | solution.py:86
  74.5 28.0 %collective-permute-start.13 = (bf16[4,48,3072]{2,1,0:T(8,128)(2,1)S(1)}, bf16[4,48,3072]{2,1,0:T(8,128)(2,1)}, u32[]{:S(2)}, u32[]{:S(2)}) collective-permute-start(bf16[4,48,3072]{2,1,0:T(8,128)(2,1)S(1)} %pad_maximum_fusion.refs_0_), channel_id=1, source_target_pairs={{16,0},{65,1},{18,2},{67,3},{20,4},{69,5},{22,6},{71,7},{24,8},{73... | collective-permute-start | bytes 3538952 | tf_op jit(solution)/shard_map/ppermute | solution.py:86
  236.8 29.1 %collective-permute-start.29 = (bf16[16,48,3072]{2,1,0:T(8,128)(2,1)}, bf16[16,48,3072]{2,1,0:T(8,128)(2,1)}, u32[]{:S(2)}, u32[]{:S(2)}) collective-permute-start(bf16[16,48,3072]{2,1,0:T(8,128)(2,1)} %get-tuple-element.44), channel_id=1, source_target_pairs={{0,1},{1,0},{2,3},{3,2},{4,5},{5,4},{6,7},{7,6},{8,9},{9,8},{10,11... | collective-permute-start | bytes 14155784 | tf_op jit(solution)/shard_map/ppermute | solution.py:86
  261.5 11.7 %collective-permute-start.23 = (bf16[4,48,1664]{2,1,0:T(8,128)(2,1)S(1)}, bf16[4,48,1664]{2,1,0:T(8,128)(2,1)S(1)}, u32[]{:S(2)}, u32[]{:S(2)}) collective-permute-start(bf16[4,48,1664]{2,1,0:T(8,128)(2,1)S(1)} %get-tuple-element.84), channel_id=1, source_target_pairs={{0,16},{1,65},{2,18},{3,67},{4,20},{5,69},{6,22},{7,71},{8,24},{9,... | collective-permute-start | bytes 1916936 | tf_op jit(solution)/shard_map/ppermute | solution.py:86
  263.2 13.0 %collective-permute-start.25 = (bf16[4,48,1664]{2,1,0:T(8,128)(2,1)S(1)}, bf16[4,48,1664]{2,1,0:T(8,128)(2,1)S(1)}, u32[]{:S(2)}, u32[]{:S(2)}) collective-permute-start(bf16[4,48,1664]{2,1,0:T(8,128)(2,1)S(1)} %get-tuple-element.85), channel_id=1, source_target_pairs={{0,48},{1,73},{2,50},{3,75},{4,52},{5,77},{6,54},{7,79},{8,56},{9,... | collective-permute-start | bytes 1916936 | tf_op jit(solution)/shard_map/ppermute | solution.py:86
  264.8 15.7 %collective-permute-start.24 = (bf16[4,48,1664]{2,1,0:T(8,128)(2,1)S(1)}, bf16[4,48,1664]{2,1,0:T(8,128)(2,1)S(1)}, u32[]{:S(2)}, u32[]{:S(2)}) collective-permute-start(bf16[4,48,1664]{2,1,0:T(8,128)(2,1)S(1)} %get-tuple-element.86), channel_id=1, source_target_pairs={{0,32},{1,9},{2,34},{3,11},{4,36},{5,13},{6,38},{7,15},{8,40},{9,1... | collective-permute-start | bytes 1916936 | tf_op jit(solution)/shard_map/ppermute | solution.py:86
  269.8 25.0 %collective-permute-start.30 = (bf16[4,48,3072]{2,1,0:T(8,128)(2,1)S(1)}, bf16[4,48,3072]{2,1,0:T(8,128)(2,1)S(1)}, u32[]{:S(2)}, u32[]{:S(2)}) collective-permute-start(bf16[4,48,3072]{2,1,0:T(8,128)(2,1)S(1)} %get-tuple-element.78), channel_id=1, source_target_pairs={{0,16},{1,65},{2,18},{3,67},{4,20},{5,69},{6,22},{7,71},{8,24},{9,... | collective-permute-start | bytes 3538952 | tf_op jit(solution)/shard_map/ppermute | solution.py:86
  270.7 27.0 %collective-permute-start.32 = (bf16[4,48,3072]{2,1,0:T(8,128)(2,1)S(1)}, bf16[4,48,3072]{2,1,0:T(8,128)(2,1)S(1)}, u32[]{:S(2)}, u32[]{:S(2)}) collective-permute-start(bf16[4,48,3072]{2,1,0:T(8,128)(2,1)S(1)} %get-tuple-element.79), channel_id=1, source_target_pairs={{0,48},{1,73},{2,50},{3,75},{4,52},{5,77},{6,54},{7,79},{8,56},{9,... | collective-permute-start | bytes 3538952 | tf_op jit(solution)/shard_map/ppermute | solution.py:86
  273.2 34.3 %collective-permute-start.31 = (bf16[4,48,3072]{2,1,0:T(8,128)(2,1)S(1)}, bf16[4,48,3072]{2,1,0:T(8,128)(2,1)S(1)}, u32[]{:S(2)}, u32[]{:S(2)}) collective-permute-start(bf16[4,48,3072]{2,1,0:T(8,128)(2,1)S(1)} %get-tuple-element.80), channel_id=1, source_target_pairs={{0,32},{1,9},{2,34},{3,11},{4,36},{5,13},{6,38},{7,15},{8,40},{9,1... | collective-permute-start | bytes 3538952 | tf_op jit(solution)/shard_map/ppermute | solution.py:86
  280.9 34.2 %collective-permute-start.26 = (bf16[48,1664]{1,0:T(8,128)(2,1)S(1)}, bf16[48,1664]{1,0:T(8,128)(2,1)S(1)}, u32[]{:S(2)}, u32[]{:S(2)}) collective-permute-start(bf16[48,1664]{1,0:T(8,128)(2,1)S(1)} %get-tuple-element.90), channel_id=1, source_target_pairs={{0,64},{1,17},{2,66},{3,19},{4,68},{5,21},{6,70},{7,23},{8,72},{9,... | collective-permute-start | bytes 479240 | tf_op jit(solution)/shard_map/ppermute | solution.py:86
  284.6 32.6 %collective-permute-start.28 = (bf16[48,1664]{1,0:T(8,128)(2,1)S(1)}, bf16[48,1664]{1,0:T(8,128)(2,1)S(1)}, u32[]{:S(2)}, u32[]{:S(2)}) collective-permute-start(bf16[48,1664]{1,0:T(8,128)(2,1)S(1)} %get-tuple-element.91), channel_id=1, source_target_pairs={{0,72},{1,49},{2,74},{3,51},{4,76},{5,53},{6,78},{7,55},{8,64},{9,... | collective-permute-start | bytes 479240 | tf_op jit(solution)/shard_map/ppermute | solution.py:86
  294.8 22.4 %collective-permute-start.27 = (bf16[48,1664]{1,0:T(8,128)(2,1)S(1)}, bf16[48,1664]{1,0:T(8,128)(2,1)S(1)}, u32[]{:S(2)}, u32[]{:S(2)}) collective-permute-start(bf16[48,1664]{1,0:T(8,128)(2,1)S(1)} %get-tuple-element.92), channel_id=1, source_target_pairs={{0,8},{1,33},{2,10},{3,35},{4,12},{5,37},{6,14},{7,39},{8,0},{9,41... | collective-permute-start | bytes 479240 | tf_op jit(solution)/shard_map/ppermute | solution.py:86
  309.2 12.6 %collective-permute-start.33 = (bf16[48,3072]{1,0:T(8,128)(2,1)}, bf16[48,3072]{1,0:T(8,128)(2,1)}, u32[]{:S(2)}, u32[]{:S(2)}) collective-permute-start(bf16[48,3072]{1,0:T(8,128)(2,1)} %get-tuple-element.87), channel_id=1, source_target_pairs={{0,64},{1,17},{2,66},{3,19},{4,68},{5,21},{6,70},{7,23},{8,72},{9,... | collective-permute-start | bytes 884744 | tf_op jit(solution)/shard_map/ppermute | solution.py:86
  314.1 10.9 %collective-permute-start.35 = (bf16[48,3072]{1,0:T(8,128)(2,1)}, bf16[48,3072]{1,0:T(8,128)(2,1)}, u32[]{:S(2)}, u32[]{:S(2)}) collective-permute-start(bf16[48,3072]{1,0:T(8,128)(2,1)} %get-tuple-element.88), channel_id=1, source_target_pairs={{0,72},{1,49},{2,74},{3,51},{4,76},{5,53},{6,78},{7,55},{8,64},{9,... | collective-permute-start | bytes 884744 | tf_op jit(solution)/shard_map/ppermute | solution.py:86
  315.1 10.2 %collective-permute-start.34 = (bf16[48,3072]{1,0:T(8,128)(2,1)}, bf16[48,3072]{1,0:T(8,128)(2,1)}, u32[]{:S(2)}, u32[]{:S(2)}) collective-permute-start(bf16[48,3072]{1,0:T(8,128)(2,1)} %get-tuple-element.89), channel_id=1, source_target_pairs={{0,8},{1,33},{2,10},{3,35},{4,12},{5,37},{6,14},{7,39},{8,0},{9,41... | collective-permute-start | bytes 884744 | tf_op jit(solution)/shard_map/ppermute | solution.py:86
  333.4 13.9 %all-to-all-start.1 = ((bf16[8,6,4736]{2,1,0:T(8,128)(2,1)}), bf16[8,6,4736]{2,1,0:T(8,128)(2,1)}, u32[]{:S(2)}, u32[]{:S(2)}) async-start(bf16[8,6,4736]{2,1,0:T(8,128)(2,1)} %pad_maximum_fusion.2), calls=%async_computation.1 | async-start | bytes 1212416 | tf_op jit(solution)/shard_map/all_to_all | solution.py:90
  (43 other events, 347.8 us)
